TPU v7x, 128 devices: a whole 4x4x4 slice. The times are simulated.
128 devices in a mesh: dp: 2 (over y_hi), expert: 64 (over z, y_lo, x, core).
Axes of the slice: x: 4, y: 4 (y_hi: 2, y_lo: 2; y = y_hi * 2 + y_lo), z: 4, core: 2. Of those that a mesh axis runs over, the one named last changes fastest.
Arguments:
- tokens: bfloat16 [2, 8192, 3584], P(None, ('dp', 'expert')), may hold values from -6 to 6
- expert_ids: int32 [2, 8192, 8], P(None, ('dp', 'expert')), may hold values from 0 to 127, all different within a row; in each aligned block of 64 rows (0 to 63, 64 to 127, ..., all dimensions but the last counted through in order) at most 5 rows name the same one
- gate_weights: float32 [2, 8192, 8], P(None, ('dp', 'expert')), may hold values from 0.05 to 0.6
- slot_expert: int32 [128], replicated, may hold values from 0 to 127, each once
- w_gate: bfloat16 [128, 3584, 1024], P(('dp', 'expert')), may hold values from -0.09375 to 0.09375
- w_up: bfloat16 [128, 3584, 1024], P(('dp', 'expert')), may hold values from -0.09375 to 0.09375
- w_down: bfloat16 [128, 1024, 3584], P(('dp', 'expert')), may hold values from -0.1875 to 0.1875
Outputs:
- mixed: bfloat16 [2, 8192, 3584], P(None, ('dp', 'expert'))
Inputs may be any that keep to these rules, and one draw needn't show every extreme that they name: `expert_ids`: in each micro-batch, the 8 ids of a token differ, and no expert is named by more than 5 of the 64 tokens of one device; some expert reaches 5. `slot_expert`: each expert lies in exactly one slot.
All inputs are finite; a program needn't handle non-finite values.
Results may differ from a plain program's by a relative error of at most 0.0057.
Values may be sent and summed in bfloat16 or wider, within the bound.
A program may use at most 192 MiB of HBM per device.

v0:
```python
import jax
import jax.numpy as jnp
from jax import lax
from jax.experimental import pallas as pl
from jax.experimental.pallas import tpu as pltpu
from jax.sharding import PartitionSpec as P

MESH = pl.DeviceIdType.MESH
BF = jnp.bfloat16
F32 = jnp.float32
I32 = jnp.int32

AXES = ((0, 1, 2), (1, 2, 0), (2, 0, 1))
CAP = 5
RING = (1, 3, 2)
LAST = tuple((dl, dc) for dl in (1, 3, 2, 0) for dc in (0, 1) if (dl, dc) != (0, 0))


def dot(a, b):
    return jnp.dot(a, b, preferred_element_type=F32)


def device_at(pos):
    z, y, x, c = pos
    return (y // 2, ((z * 2 + y % 2) * 4 + x) * 2 + c)


def moved(pos, axis, by, core=0):
    out = list(pos)
    out[axis] = (pos[axis] + by) % 4
    if core:
        out[3] = 1 - pos[3]
    return tuple(out)


def kernel(
    sizes, tokens, ids, gates, slots, w_gate, w_up, w_down, out,
    tok_all, stage, mid, last, fin, info, hidden, hid_f, pick, comb, swap, rot, rot_t,
    wgu, wd, sem_send, sem_recv, sem_local, sem_info_s, sem_info_r, sem_w, sem_wd, free_mid, free_last,
):
    batches, rows_tok, _ = tokens.shape
    starts, widths, tile, tiles = sizes
    dp = lax.axis_index("dp")
    ex = lax.axis_index("expert")
    pos = (ex // 16, dp * 2 + (ex // 8) % 2, (ex // 2) % 4, ex % 2)

    def cols(f):
        return pl.ds(starts[f], widths[f])

    def block(i, n):
        return pl.ds(pl.multiple_of(i * n, n), n)

    peers = [(a, by, c) for a in range(3) for by in (1, 2, 3) for c in (0, 1)] + [(0, 0, 1)]
    barrier = pltpu.get_barrier_semaphore()
    for a, by, c in peers:
        pl.semaphore_signal(barrier, inc=1, device_id=device_at(moved(pos, a, by, c)), device_id_type=MESH)
    pl.semaphore_wait(barrier, len(peers))

    def remote(src, dst, m, f, send, recv, target):
        return pltpu.make_async_remote_copy(
            src_ref=src, dst_ref=dst, send_sem=sem_send.at[m, f, send], recv_sem=sem_recv.at[m, f, recv],
            device_id=device_at(target), device_id_type=MESH,
        )

    def own(src, dst, m, f):
        return pltpu.make_async_copy(src, dst, sem_local.at[m, f])

    def once(make):
        held = {}

        def get(m, f):
            if (m, f) not in held:
                held[m, f] = make(m, f)
            return held[m, f]

        return get

    @once
    def phase1(m, f):
        b = AXES[f][0]
        src = tokens.at[m, :, cols(f)]
        dst = tok_all.at[m, pos[b], :, cols(f)]
        far = [remote(src, dst, m, f, i, i, moved(pos, b, by)) for i, by in enumerate(RING)]
        return far, own(src, dst, m, f)

    def along_mid(m, f, base):
        a = AXES[f][1]

        def src(to):
            return stage.at[m, block(to, 160), cols(f)]

        dst = mid.at[m, block(pos[a], 160), cols(f)]
        far = [
            remote(src((pos[a] + by) % 4), dst, m, f, i, base + i, moved(pos, a, by)) for i, by in enumerate(RING)
        ]
        return far, own(src(pos[a]), dst, m, f)

    def along_last(m, f, base):
        a = AXES[f][2]

        def src(to, core):
            return stage.at[m, block(core * 4 + to, 80), cols(f)]

        dst = last.at[m, block(pos[3] * 4 + pos[a], 80), cols(f)]
        far = [
            remote(
                src((pos[a] + by) % 4, 1 - pos[3] if dc else pos[3]), dst, m, f, i, base + i, moved(pos, a, by, dc)
            )
            for i, (by, dc) in enumerate(LAST)
        ]
        return far, own(src(pos[a], pos[3]), dst, m, f)

    @once
    def phase2(m, f):
        return along_mid(m, f, 3)

    @once
    def phase3(m, f):
        return along_last(m, f, 6)

    @once
    def back3(m, f):
        return along_last(m, f, 13)

    @once
    def back2(m, f):
        return along_mid(m, f, 20)

    @once
    def back1(m, f):
        b = AXES[f][0]
        far = [
            remote(
                tok_all.at[m, (pos[b] + by) % 4, :, cols(f)], fin.at[m, i, :, cols(f)], m, f, i, 23 + i,
                moved(pos, b, by),
            )
            for i, by in enumerate(RING)
        ]
        return far, None

    def start(copies):
        far, near = copies
        for copy in far:
            copy.start()
        if near is not None:
            near.start()

    def arrive(copies):
        far, near = copies
        for copy in far:
            copy.wait_recv()
        if near is not None:
            near.wait()

    def sent(copies):
        for copy in copies[0]:
            copy.wait_send()

    def load_tile(j, slot):
        at = pl.ds(pl.multiple_of(j * tile, tile), tile)
        return (
            pltpu.make_async_copy(w_gate.at[0, :, at], wgu.at[slot, 0], sem_w.at[slot, 0]),
            pltpu.make_async_copy(w_up.at[0, :, at], wgu.at[slot, 1], sem_w.at[slot, 1]),
        )

    for m in range(batches):
        for f in range(3):
            start(phase1(m, f))
    load_down = pltpu.make_async_copy(w_down.at[0], wd, sem_wd)
    load_down.start()
    for slot in range(2):
        for copy in load_tile(slot, slot):
            copy.start()

    sub = lax.broadcasted_iota(I32, (128, 128), 0)
    lane = lax.broadcasted_iota(I32, (128, 128), 1)
    holder = jnp.sum(jnp.where(slots[...] == sub, lane, 0).astype(F32), axis=1, keepdims=True) * 8.0
    before = jnp.where((sub < 64) & (sub < lane % 64), 1.0, 0.0).astype(BF)
    lane8 = lax.broadcasted_iota(I32, (8, 128), 1)
    for m in range(batches):
        names = ids[m]
        same = [names[k : k + 1, :] == sub for k in range(8)]
        chosen = jnp.where(same[0], 1.0, 0.0)
        for k in range(1, 8):
            chosen = chosen + jnp.where(same[k], 1.0, 0.0)
        value = dot(chosen.astype(BF), before) + holder
        found = jnp.concatenate(
            [jnp.sum(jnp.where(same[k], value, 0.0), axis=0, keepdims=True) for k in range(8)], axis=0
        ).astype(I32)
        rank = found & 7
        where = found >> 3
        at = (
            (where >> 4) & 3,
            ((where >> 3) & 1) + ((where >> 6) & 1) * 2,
            (where >> 1) & 3,
            where & 1,
        )
        for f in range(3):
            b, a, l = AXES[f]
            key = at[b] * 640 + at[a] * 160 + (at[3] * 4 + at[l]) * 20 + pos[b] * CAP + rank
            mine = (lane8 >= 64) == (lax.broadcast(pos[b] % 2, (8, 128)) == 1)
            info[f, pos[b], m, 0:8, :] = jnp.where(mine, key.astype(F32), -1.0)
            info[f, pos[b], m, 8:16, :] = jnp.where(mine, gates[m], 0.0)
    tell = []
    for f in range(3):
        b = AXES[f][0]
        for i, by in enumerate(RING):
            tell.append(
                pltpu.make_async_remote_copy(
                    src_ref=info.at[f, pos[b]], dst_ref=info.at[f, pos[b]], send_sem=sem_info_s.at[f, i],
                    recv_sem=sem_info_r.at[f, i], device_id=device_at(moved(pos, b, by)), device_id_type=MESH,
                )
            )
    for copy in tell:
        copy.start()

    r = lax.broadcasted_iota(I32, (320, 320), 0)
    n = lax.broadcasted_iota(I32, (320, 320), 1)
    fifth = (r * 205) >> 10
    d0, d1, d2, d3 = fifth >> 4, (fifth >> 2) & 3, fifth & 3, r - fifth * 5
    swap[...] = jnp.where(n == d1 * 80 + d0 * 20 + d2 * 5 + d3, 1.0, 0.0).astype(BF)
    rot[...] = jnp.where(n == d2 * 80 + d0 * 20 + d1 * 5 + d3, 1.0, 0.0).astype(BF)
    rot_t[...] = jnp.where(n == d1 * 80 + d2 * 20 + d0 * 5 + d3, 1.0, 0.0).astype(BF)

    for copy in tell:
        copy.wait()

    def keys(m, f):
        low = jnp.maximum(info[f, 0, m, 0:8, :], info[f, 1, m, 0:8, :])
        high = jnp.maximum(info[f, 2, m, 0:8, :], info[f, 3, m, 0:8, :])
        return jnp.concatenate([low, high], axis=1)

    def weights(m, f):
        low = info[f, 0, m, 8:16, :] + info[f, 1, m, 8:16, :]
        high = info[f, 2, m, 8:16, :] + info[f, 3, m, 8:16, :]
        return jnp.concatenate([low, high], axis=1)

    def row_key(f, i):
        return (lax.broadcasted_iota(I32, (128, 256), 0) + (pos[AXES[f][0]] * 640 + i * 128)).astype(F32)

    def build_pick(m, f):
        key = keys(m, f)
        for i in range(5):
            row = row_key(f, i)
            hit = key[0:1, :] == row
            for k in range(1, 8):
                hit = hit | (key[k : k + 1, :] == row)
            pick[i * 128 : (i + 1) * 128, :] = jnp.where(hit, 1.0, 0.0).astype(BF)

    def build_comb(m, f):
        key = keys(m, f)
        gate = weights(m, f)
        for i in range(5):
            row = row_key(f, i)
            total = jnp.zeros((128, 256), F32)
            for k in range(8):
                total = jnp.where(key[k : k + 1, :] == row, gate[k : k + 1, :], total)
            comb[m, f, :, i * 128 : (i + 1) * 128] = total.T.astype(BF)

    def chunks(f):
        at = 0
        while at < widths[f]:
            size = min(512, widths[f] - at)
            yield starts[f] + at, size
            at += size

    def step1(m, f):
        build_pick(m, f)
        arrive(phase1(m, f))
        for at, size in chunks(f):
            rows = tok_all[m, :, :, at : at + size].reshape(4 * rows_tok, size)
            stage[m, :, at : at + size] = dot(pick[...], rows).astype(BF)
        sent(phase1(m, f))
        start(phase2(m, f))

    def step2(m, f):
        arrive(phase2(m, f))
        sent(phase2(m, f))
        for at, size in chunks(f):
            for c in range(2):
                rows = jnp.concatenate(
                    [mid[m, i * 160 + c * 80 : i * 160 + c * 80 + 80, at : at + size] for i in range(4)], axis=0
                )
                stage[m, c * 320 : c * 320 + 320, at : at + size] = dot(swap[...], rows).astype(BF)
        for by in RING:
            pl.semaphore_signal(
                free_mid.at[m, f], inc=1, device_id=device_at(moved(pos, AXES[f][1], by)), device_id_type=MESH
            )
        start(phase3(m, f))

    def gather(m, f):
        arrive(phase3(m, f))
        sent(phase3(m, f))
        for at, size in chunks(f):
            for c in range(2):
                rows = last[m, c * 320 : c * 320 + 320, at : at + size]
                if f:
                    rows = dot((rot, rot_t)[f - 1][...], rows).astype(BF)
                stage[m, c * 320 : c * 320 + 320, at : at + size] = rows
        for by, dc in LAST:
            pl.semaphore_signal(
                free_last.at[m, f], inc=1, device_id=device_at(moved(pos, AXES[f][2], by, dc)), device_id_type=MESH
            )

    def expand(m):
        def one(j, carry):
            slot = j % 2
            for copy in load_tile(j, slot):
                copy.wait()

            def half(i, carry):
                at = pl.ds(pl.multiple_of(i * 320, 320), 320)
                rows = stage[m, at, :]
                gate = dot(rows, wgu[slot, 0])
                up = dot(rows, wgu[slot, 1])
                hidden[at, pl.ds(pl.multiple_of(j * tile, tile), tile)] = (gate / (1.0 + jnp.exp(-gate)) * up).astype(BF)
                return carry

            lax.fori_loop(0, 2, half, 0)
            following = j + 2 if m + 1 == batches else (j + 2) % tiles

            def more():
                for copy in load_tile(following, slot):
                    copy.start()

            if m + 1 == batches:
                pl.when(following < tiles)(more)
            else:
                more()
            return carry

        lax.fori_loop(0, tiles, one, 0)

    def shrink(m, f):
        if f:
            for c in range(2):
                hid_f[c * 320 : c * 320 + 320, :] = dot(
                    (rot_t, rot)[f - 1][...], hidden[c * 320 : c * 320 + 320, :]
                ).astype(BF)
        rows = (hid_f if f else hidden)[...]
        for at, size in chunks(f):
            stage[m, :, at : at + size] = dot(rows, wd[:, at : at + size]).astype(BF)
        pl.semaphore_wait(free_last.at[m, f], len(LAST))
        start(back3(m, f))

    def step4(m, f):
        arrive(back3(m, f))
        sent(back3(m, f))
        for at, size in chunks(f):
            for c in range(2):
                rows = dot(swap[...], last[m, c * 320 : c * 320 + 320, at : at + size]).astype(BF)
                for i in range(4):
                    stage[m, i * 160 + c * 80 : i * 160 + c * 80 + 80, at : at + size] = rows[i * 80 : i * 80 + 80, :]
        pl.semaphore_wait(free_mid.at[m, f], len(RING))
        start(back2(m, f))

    def step5(m, f):
        arrive(back2(m, f))
        sent(back2(m, f))
        for at, size in chunks(f):
            rows = dot(comb[m, f], mid[m, :, at : at + size]).astype(BF)
            tok_all[m, :, :, at : at + size] = rows.reshape(4, rows_tok, size)
        start(back1(m, f))

    def step6(m, f):
        arrive(back1(m, f))
        total = tok_all[m, pos[AXES[f][0]], :, cols(f)].astype(F32)
        for i in range(3):
            total = total + fin[m, i, :, cols(f)].astype(F32)
        out[m, :, cols(f)] = total.astype(BF)
        sent(back1(m, f))

    parts = range(3)
    for m in range(batches):
        for f in parts:
            step1(m, f)
    for m in range(batches):
        for f in parts:
            build_comb(m, f)
    for m in range(batches):
        for f in parts:
            step2(m, f)
    load_down.wait()
    for m in range(batches):
        for f in parts:
            gather(m, f)
        expand(m)
        for f in parts:
            shrink(m, f)
    for m in range(batches):
        for f in parts:
            step4(m, f)
    for m in range(batches):
        for f in parts:
            step5(m, f)
    for m in range(batches):
        for f in parts:
            step6(m, f)


def local(tokens, expert_ids, gate_weights, slot_expert, w_gate, w_up, w_down):
    batches, rows, width = tokens.shape
    ff = w_gate.shape[2]
    slots = 128 * CAP
    unit = width // 128
    widths = (unit // 3 * 128, unit // 3 * 128, (unit - 2 * (unit // 3)) * 128)
    starts = (0, widths[0], widths[0] + widths[1])
    tile = 256
    tiles = ff // tile

    def lanes(a):
        turned = jnp.swapaxes(a, 1, 2)
        return jnp.concatenate([turned, turned], axis=2)

    vmem = pl.BlockSpec(memory_space=pltpu.VMEM)
    hbm = pl.BlockSpec(memory_space=pl.ANY)

    def body(*refs):
        kernel((starts, widths, tile, tiles), *refs)

    return pl.pallas_call(
        body,
        out_shape=jax.ShapeDtypeStruct(tokens.shape, BF),
        in_specs=[hbm, vmem, vmem, vmem, hbm, hbm, hbm],
        out_specs=vmem,
        scratch_shapes=[
            pltpu.VMEM((batches, 4, rows, width), BF),
            pltpu.VMEM((batches, slots, width), BF),
            pltpu.VMEM((batches, slots, width), BF),
            pltpu.VMEM((batches, slots, width), BF),
            pltpu.VMEM((batches, 3, rows, width), BF),
            pltpu.VMEM((3, 4, batches, 16, 128), F32),
            pltpu.VMEM((slots, ff), BF),
            pltpu.VMEM((slots, ff), BF),
            pltpu.VMEM((slots, 4 * rows), BF),
            pltpu.VMEM((batches, 3, 4 * rows, slots), BF),
            pltpu.VMEM((320, 320), BF),
            pltpu.VMEM((320, 320), BF),
            pltpu.VMEM((320, 320), BF),
            pltpu.VMEM((2, 2, width, tile), BF),
            pltpu.VMEM((ff, width), BF),
            pltpu.SemaphoreType.DMA((batches, 3, 7)),
            pltpu.SemaphoreType.DMA((batches, 3, 26)),
            pltpu.SemaphoreType.DMA((batches, 3)),
            pltpu.SemaphoreType.DMA((3, 3)),
            pltpu.SemaphoreType.DMA((3, 3)),
            pltpu.SemaphoreType.DMA((2, 2)),
            pltpu.SemaphoreType.DMA,
            pltpu.SemaphoreType.REGULAR((batches, 3)),
            pltpu.SemaphoreType.REGULAR((batches, 3)),
        ],
        compiler_params=pltpu.CompilerParams(collective_id=0, has_side_effects=True, vmem_limit_bytes=62 << 20),
        cost_estimate=pl.CostEstimate(flops=60 * 10**9, bytes_accessed=24 * 10**6, transcendentals=10**6),
    )(tokens, lanes(expert_ids), lanes(gate_weights), slot_expert.reshape(1, -1), w_gate, w_up, w_down)


def solution(mesh):
    in_specs = (
        P(None, ("dp", "expert"), None),
        P(None, ("dp", "expert"), None),
        P(None, ("dp", "expert"), None),
        P(),
        P(("dp", "expert"), None, None),
        P(("dp", "expert"), None, None),
        P(("dp", "expert"), None, None),
    )
    out_specs = P(None, ("dp", "expert"), None)
    return jax.shard_map(local, mesh=mesh, in_specs=in_specs, out_specs=out_specs, check_vma=False)
```

profile of v0, /device:TPU:1, one launch (start us, length us, event | category | flops | bytes accessed | tf_op | source)
XLA Modules:
  0.0 199.5 jit_solution(14569554676021473963)
XLA Ops:
  0.0 1.4 pad_add_fusion.refs_1_
  1.4 1.4 pad_maximum_fusion.refs_2_
  2.9 194.1 %shard_map.73 = bf16[2,64,3584]{2,1,0:T(8,128)(2,1)} custom-call(bf16[2,64,3584]{2,1,0:T(8,128)(2,1)} %refs_0_.1, s32[2,8,128]{2,1,0:T(8,128)} %pad_add_fusion.refs_1_, f32[2,8,128]{2,1,0:T(8,128)} %pad_maximum_fusion.refs_2_, s32[1,128]{1,0:T(1,128)} %bitcast.5, bf16[1,3584,1024]{2,1,0:T(8,128)(2,1)} %refs_4_.1, bf16[1,3584,1024]{2,1,0:T(8,128)(2,1)} %refs_5_.1, ...), custom_call_target="tpu_custom_call" | custom-call | flops 60000002048 | bytes 24000000 | tf_op jit(solution)/shard_map/pallas_call | solution.py:421
  197.0 2.2 %copy.9 = bf16[2,64,3584]{2,1,0:T(8,128)(2,1)} copy(bf16[2,64,3584]{2,1,0:T(8,128)(2,1)} %shard_map.73) | data formatting | bytes 1835008
where the time goes:
time: 202 us; the launch traced here: 199 us
  Pallas kernels  194 us (96%)
  other arithmetic  2.88 us (1%)
  local copies, waits for them, and re-layouts  2.16 us (1%)
    pallas_call x1, Pallas kernels, local(): pl.pallas_call(body, out_shape=jax.ShapeDtypeStruct(tokens.shape, BF), in...  194 us

commit v1 on v0

v1 whole, which is shorter than its diff:
```python
import jax
import jax.numpy as jnp
from jax import lax
from jax.experimental import pallas as pl
from jax.experimental.pallas import tpu as pltpu
from jax.sharding import PartitionSpec as P

MESH = pl.DeviceIdType.MESH
BF = jnp.bfloat16
F32 = jnp.float32
I32 = jnp.int32

AXES = ((0, 1, 2), (1, 2, 0), (2, 0, 1))
CAP = 5
RING = (1, 3, 2)
LAST = tuple((dl, dc) for dl in (1, 3, 2, 0) for dc in (0, 1) if (dl, dc) != (0, 0))


def dot(a, b):
    return jnp.dot(a, b, preferred_element_type=F32)


def device_at(pos):
    z, y, x, c = pos
    return (y // 2, ((z * 2 + y % 2) * 4 + x) * 2 + c)


def moved(pos, axis, by, core=0):
    out = list(pos)
    out[axis] = (pos[axis] + by) % 4
    if core:
        out[3] = 1 - pos[3]
    return tuple(out)


def kernel(
    sizes, tokens, ids, gates, slots, w_gate, w_up, w_down, out,
    tok_all, stage, mid, last, fin, info, hidden, pick, comb, swap, rot, rot_t,
    wg, wu, wd, sem_send, sem_recv, sem_local, sem_info_s, sem_info_r, sem_w, free_mid, free_last,
):
    batches, rows_tok, _ = tokens.shape
    starts, widths, tile, tiles = sizes
    dp = lax.axis_index("dp")
    ex = lax.axis_index("expert")
    pos = (ex // 16, dp * 2 + (ex // 8) % 2, (ex // 2) % 4, ex % 2)

    def cols(f):
        return pl.ds(starts[f], widths[f])

    def block(i, n):
        return pl.ds(pl.multiple_of(i * n, n), n)

    peers = [(a, by, c) for a in range(3) for by in (1, 2, 3) for c in (0, 1)] + [(0, 0, 1)]
    barrier = pltpu.get_barrier_semaphore()
    for a, by, c in peers:
        pl.semaphore_signal(barrier, inc=1, device_id=device_at(moved(pos, a, by, c)), device_id_type=MESH)
    sub = lax.broadcasted_iota(I32, (128, 128), 0)
    lane = lax.broadcasted_iota(I32, (128, 128), 1)
    holder = jnp.sum(jnp.where(slots[...] == sub, lane, 0).astype(F32), axis=1, keepdims=True) * 8.0
    before = jnp.where((sub < 64) & (sub < lane % 64), 1.0, 0.0).astype(BF)
    lane8 = lax.broadcasted_iota(I32, (8, 128), 1)
    twice = jnp.where(sub[:64] == lane[:64] % 64, 1.0, 0.0).astype(BF)

    def turned(rows):
        return lax.dot_general(rows.astype(BF), twice, (((0,), (0,)), ((), ())), preferred_element_type=F32)

    for m in range(batches):
        names = turned(ids[m].astype(F32)).astype(I32)
        gate_rows = turned(gates[m])
        same = [names[k : k + 1, :] == sub for k in range(8)]
        chosen = jnp.where(same[0], 1.0, 0.0)
        for k in range(1, 8):
            chosen = chosen + jnp.where(same[k], 1.0, 0.0)
        value = dot(chosen.astype(BF), before) + holder
        found = jnp.concatenate(
            [jnp.sum(jnp.where(same[k], value, 0.0), axis=0, keepdims=True) for k in range(8)], axis=0
        ).astype(I32)
        rank = found & 7
        where = found >> 3
        at = (
            (where >> 4) & 3,
            ((where >> 3) & 1) + ((where >> 6) & 1) * 2,
            (where >> 1) & 3,
            where & 1,
        )
        for f in range(3):
            b, a, l = AXES[f]
            key = at[b] * 640 + at[a] * 160 + (at[3] * 4 + at[l]) * 20 + pos[b] * CAP + rank
            mine = (lane8 >= 64) == (lax.broadcast(pos[b] % 2, (8, 128)) == 1)
            info[f, pos[b], m, 0:8, :] = jnp.where(mine, key.astype(F32), -1.0)
            info[f, pos[b], m, 8:16, :] = jnp.where(mine, gate_rows, 0.0)
    pl.semaphore_wait(barrier, len(peers))

    def remote(src, dst, m, f, send, recv, target):
        return pltpu.make_async_remote_copy(
            src_ref=src, dst_ref=dst, send_sem=sem_send.at[m, f, send], recv_sem=sem_recv.at[m, f, recv],
            device_id=device_at(target), device_id_type=MESH,
        )

    def own(src, dst, m, f):
        return pltpu.make_async_copy(src, dst, sem_local.at[m, f])

    def once(make):
        held = {}

        def get(m, f):
            if (m, f) not in held:
                held[m, f] = make(m, f)
            return held[m, f]

        return get

    @once
    def phase1(m, f):
        b = AXES[f][0]
        src = tokens.at[m, :, cols(f)]
        dst = tok_all.at[m, pos[b], :, cols(f)]
        far = [remote(src, dst, m, f, i, i, moved(pos, b, by)) for i, by in enumerate(RING)]
        return far, own(src, dst, m, f)

    def along_mid(m, f, base):
        a = AXES[f][1]

        def src(to):
            return stage.at[m, block(to, 160), cols(f)]

        dst = mid.at[m, block(pos[a], 160), cols(f)]
        far = [
            remote(src((pos[a] + by) % 4), dst, m, f, i, base + i, moved(pos, a, by)) for i, by in enumerate(RING)
        ]
        return far, own(src(pos[a]), dst, m, f)

    def along_last(m, f, base):
        a = AXES[f][2]

        def src(to, core):
            return stage.at[m, block(core * 4 + to, 80), cols(f)]

        dst = last.at[m, block(pos[3] * 4 + pos[a], 80), cols(f)]
        far = [
            remote(
                src((pos[a] + by) % 4, 1 - pos[3] if dc else pos[3]), dst, m, f, i, base + i, moved(pos, a, by, dc)
            )
            for i, (by, dc) in enumerate(LAST)
        ]
        return far, own(src(pos[a], pos[3]), dst, m, f)

    @once
    def phase2(m, f):
        return along_mid(m, f, 3)

    @once
    def phase3(m, f):
        return along_last(m, f, 6)

    @once
    def back3(m, f):
        return along_last(m, f, 13)

    @once
    def back2(m, f):
        return along_mid(m, f, 20)

    @once
    def back1(m, f):
        b = AXES[f][0]
        far = [
            remote(
                tok_all.at[m, (pos[b] + by) % 4, :, cols(f)], fin.at[m, i, :, cols(f)], m, f, i, 23 + i,
                moved(pos, b, by),
            )
            for i, by in enumerate(RING)
        ]
        return far, None

    def start(copies):
        far, near = copies
        for copy in far:
            copy.start()
        if near is not None:
            near.start()

    def arrive(copies):
        far, near = copies
        for copy in far:
            copy.wait_recv()
        if near is not None:
            near.wait()

    def sent(copies):
        for copy in copies[0]:
            copy.wait_send()

    tell = []
    for f in range(3):
        b = AXES[f][0]
        for i, by in enumerate(RING):
            tell.append(
                pltpu.make_async_remote_copy(
                    src_ref=info.at[f, pos[b]], dst_ref=info.at[f, pos[b]], send_sem=sem_info_s.at[f, i],
                    recv_sem=sem_info_r.at[f, i], device_id=device_at(moved(pos, b, by)), device_id_type=MESH,
                )
            )
    for copy in tell:
        copy.start()

    for m in range(batches):
        for f in range(3):
            start(phase1(m, f))
    loads = [
        pltpu.make_async_copy(src.at[0], dst, sem_w.at[i])
        for i, (src, dst) in enumerate(((w_gate, wg), (w_up, wu), (w_down, wd)))
    ]
    for copy in loads:
        copy.start()

    r = lax.broadcasted_iota(I32, (320, 320), 0)
    n = lax.broadcasted_iota(I32, (320, 320), 1)
    fifth = (r * 205) >> 10
    d0, d1, d2, d3 = fifth >> 4, (fifth >> 2) & 3, fifth & 3, r - fifth * 5
    swap[...] = jnp.where(n == d1 * 80 + d0 * 20 + d2 * 5 + d3, 1.0, 0.0).astype(BF)
    rot[...] = jnp.where(n == d2 * 80 + d0 * 20 + d1 * 5 + d3, 1.0, 0.0).astype(BF)
    rot_t[...] = jnp.where(n == d1 * 80 + d2 * 20 + d0 * 5 + d3, 1.0, 0.0).astype(BF)

    for copy in tell:
        copy.wait()

    def keys(m, f):
        low = jnp.maximum(info[f, 0, m, 0:8, :], info[f, 1, m, 0:8, :])
        high = jnp.maximum(info[f, 2, m, 0:8, :], info[f, 3, m, 0:8, :])
        return jnp.concatenate([low, high], axis=1)

    def weights(m, f):
        low = info[f, 0, m, 8:16, :] + info[f, 1, m, 8:16, :]
        high = info[f, 2, m, 8:16, :] + info[f, 3, m, 8:16, :]
        return jnp.concatenate([low, high], axis=1)

    def row_key(f, i):
        return (lax.broadcasted_iota(I32, (128, 256), 0) + (pos[AXES[f][0]] * 640 + i * 128)).astype(F32)

    def build_pick(m, f):
        key = keys(m, f)
        for i in range(5):
            row = row_key(f, i)
            hit = key[0:1, :] == row
            for k in range(1, 8):
                hit = hit | (key[k : k + 1, :] == row)
            pick[i * 128 : (i + 1) * 128, :] = jnp.where(hit, 1.0, 0.0).astype(BF)

    def build_comb(m, f):
        key = keys(m, f)
        gate = weights(m, f)
        for i in range(5):
            row = row_key(f, i)
            total = jnp.zeros((128, 256), F32)
            for k in range(8):
                total = jnp.where(key[k : k + 1, :] == row, gate[k : k + 1, :], total)
            comb[m, f, :, i * 128 : (i + 1) * 128] = total.T.astype(BF)

    def halves(work):
        def one(c, carry):
            work(c)
            return carry

        lax.fori_loop(0, 2, one, 0)

    def chunks(f):
        at = 0
        while at < widths[f]:
            size = min(512, widths[f] - at)
            yield starts[f] + at, size
            at += size

    def step1(m, f):
        build_pick(m, f)
        phase1(m, f)[1].wait()
        arrive((phase1(m, f)[0], None))
        for at, size in chunks(f):
            rows = tok_all[m, :, :, at : at + size].reshape(4 * rows_tok, size)
            stage[m, :, at : at + size] = dot(pick[...], rows).astype(BF)
        sent(phase1(m, f))
        start(phase2(m, f))

    def step2(m, f):
        arrive(phase2(m, f))
        sent(phase2(m, f))
        @halves
        def _(c):
            for at, size in chunks(f):
                rows = jnp.concatenate(
                    [mid[m, block(i * 2 + c, 80), at : at + size] for i in range(4)], axis=0
                )
                stage[m, block(c, 320), at : at + size] = dot(swap[...], rows).astype(BF)

        for by in RING:
            pl.semaphore_signal(
                free_mid.at[m, f], inc=1, device_id=device_at(moved(pos, AXES[f][1], by)), device_id_type=MESH
            )
        start(phase3(m, f))

    def side(copies, h):
        return [copy for copy, (by, dc) in zip(copies[0], LAST) if dc == h], None if h else copies[1]

    def half(h):
        return block(1 - pos[3] if h else pos[3], 320)

    def gather(m, f, h):
        arrive(side(phase3(m, f), h))
        if h == 0:
            sent(phase3(m, f))
        for at, size in chunks(f):
            rows = last[m, half(h), at : at + size]
            if f:
                rows = dot((rot, rot_t)[f - 1][...], rows).astype(BF)
            stage[m, half(h), at : at + size] = rows
        for by, dc in LAST:
            if dc == h:
                pl.semaphore_signal(
                    free_last.at[m, f, h], inc=1, device_id=device_at(moved(pos, AXES[f][2], by, dc)),
                    device_id_type=MESH,
                )

    def expand(m, h):
        def one(j, carry):
            at = pl.ds(pl.multiple_of(j * tile, tile), tile)
            rows = stage[m, half(h), :]
            gate = dot(rows, wg[:, at])
            up = dot(rows, wu[:, at])
            hidden[:, at] = (gate / (1.0 + jnp.exp(-gate)) * up).astype(BF)
            return carry

        lax.fori_loop(0, tiles, one, 0)

    def shrink(m, f, h):
        rows = hidden[...]
        if f:
            rows = dot((rot_t, rot)[f - 1][...], rows).astype(BF)
        for at, size in chunks(f):
            stage[m, half(h), at : at + size] = dot(rows, wd[:, at : at + size]).astype(BF)
        pl.semaphore_wait(free_last.at[m, f, h], 3 + h)
        start(side(back3(m, f), h))

    def step4(m, f):
        arrive(back3(m, f))
        sent(back3(m, f))
        @halves
        def _(c):
            for at, size in chunks(f):
                rows = dot(swap[...], last[m, block(c, 320), at : at + size]).astype(BF)
                for i in range(4):
                    stage[m, block(i * 2 + c, 80), at : at + size] = rows[i * 80 : i * 80 + 80, :]

        pl.semaphore_wait(free_mid.at[m, f], len(RING))
        start(back2(m, f))

    def step5(m, f):
        arrive(back2(m, f))
        sent(back2(m, f))
        for at, size in chunks(f):
            rows = dot(comb[m, f], mid[m, :, at : at + size]).astype(BF)
            tok_all[m, :, :, at : at + size] = rows.reshape(4, rows_tok, size)
        start(back1(m, f))

    @once
    def leave(m, f):
        return own(tok_all.at[m, pos[AXES[f][0]], :, cols(f)], out.at[m, :, cols(f)], m, f)

    def step6(m, f):
        arrive(back1(m, f))
        total = tok_all[m, pos[AXES[f][0]], :, cols(f)].astype(F32)
        for i in range(3):
            total = total + fin[m, i, :, cols(f)].astype(F32)
        tok_all[m, pos[AXES[f][0]], :, cols(f)] = total.astype(BF)
        leave(m, f).start()
        sent(back1(m, f))

    parts = range(3)
    for f in parts:
        step1(0, f)
    for f in parts:
        step1(1, f)
    for f in parts:
        build_comb(0, f)
    for f in parts:
        build_comb(1, f)
    for f in parts:
        step2(0, f)
    for f in parts:
        step2(1, f)
    for copy in loads:
        copy.wait()
    for f in parts:
        gather(0, f, 0)
    expand(0, 0)
    for f in parts:
        shrink(0, f, 0)
    for f in parts:
        gather(0, f, 1)
    expand(0, 1)
    for f in parts:
        shrink(0, f, 1)
    for f in parts:
        gather(1, f, 0)
    expand(1, 0)
    for f in parts:
        shrink(1, f, 0)
    for f in parts:
        gather(1, f, 1)
    expand(1, 1)
    for f in parts:
        shrink(1, f, 1)
    for f in parts:
        step4(0, f)
    for f in parts:
        step4(1, f)
    for f in parts:
        step5(0, f)
    for f in parts:
        step5(1, f)
    for f in parts:
        step6(0, f)
    for f in parts:
        step6(1, f)
    for f in parts:
        leave(0, f).wait()
    for f in parts:
        leave(1, f).wait()


def local(tokens, expert_ids, gate_weights, slot_expert, w_gate, w_up, w_down):
    batches, rows, width = tokens.shape
    ff = w_gate.shape[2]
    slots = 128 * CAP
    unit = width // 128
    widths = (unit // 3 * 128, unit // 3 * 128, (unit - 2 * (unit // 3)) * 128)
    starts = (0, widths[0], widths[0] + widths[1])
    tile = 256
    tiles = ff // tile

    vmem = pl.BlockSpec(memory_space=pltpu.VMEM)
    hbm = pl.BlockSpec(memory_space=pl.ANY)

    def body(*refs):
        kernel((starts, widths, tile, tiles), *refs)

    return pl.pallas_call(
        body,
        out_shape=jax.ShapeDtypeStruct(tokens.shape, BF),
        in_specs=[hbm, vmem, vmem, vmem, hbm, hbm, hbm],
        out_specs=hbm,
        scratch_shapes=[
            pltpu.VMEM((batches, 4, rows, width), BF),
            pltpu.VMEM((batches, slots, width), BF),
            pltpu.VMEM((batches, slots, width), BF),
            pltpu.VMEM((batches, slots, width), BF),
            pltpu.VMEM((batches, 3, rows, width), BF),
            pltpu.VMEM((3, 4, batches, 16, 128), F32),
            pltpu.VMEM((slots // 2, ff), BF),
            pltpu.VMEM((slots, 4 * rows), BF),
            pltpu.VMEM((batches, 3, 4 * rows, slots), BF),
            pltpu.VMEM((320, 320), BF),
            pltpu.VMEM((320, 320), BF),
            pltpu.VMEM((320, 320), BF),
            pltpu.VMEM((width, ff), BF),
            pltpu.VMEM((width, ff), BF),
            pltpu.VMEM((ff, width), BF),
            pltpu.SemaphoreType.DMA((batches, 3, 7)),
            pltpu.SemaphoreType.DMA((batches, 3, 26)),
            pltpu.SemaphoreType.DMA((batches, 3)),
            pltpu.SemaphoreType.DMA((3, 3)),
            pltpu.SemaphoreType.DMA((3, 3)),
            pltpu.SemaphoreType.DMA((3,)),
            pltpu.SemaphoreType.REGULAR((batches, 3)),
            pltpu.SemaphoreType.REGULAR((batches, 3, 2)),
        ],
        compiler_params=pltpu.CompilerParams(collective_id=0, has_side_effects=True, vmem_limit_bytes=62 << 20),
        cost_estimate=pl.CostEstimate(flops=60 * 10**9, bytes_accessed=24 * 10**6, transcendentals=10**6),
    )(tokens, expert_ids, gate_weights, slot_expert.reshape(1, -1), w_gate, w_up, w_down)


def solution(mesh):
    in_specs = (
        P(None, ("dp", "expert"), None),
        P(None, ("dp", "expert"), None),
        P(None, ("dp", "expert"), None),
        P(),
        P(("dp", "expert"), None, None),
        P(("dp", "expert"), None, None),
        P(("dp", "expert"), None, None),
    )
    out_specs = P(None, ("dp", "expert"), None)
    return jax.shard_map(local, mesh=mesh, in_specs=in_specs, out_specs=out_specs, check_vma=False)
```

time: 202 us -> 184 us (0.911)
  the two profiles are of different devices: /device:TPU:1 before, /device:TPU:0 now
where the time goes in v1:
time: 184 us; the launch traced here: 181 us
  Pallas kernels  176 us (96%)
  local copies, waits for them, and re-layouts  5 us (3%)
    pallas_call x1, Pallas kernels, local(): pl.pallas_call(body, out_shape=jax.ShapeDtypeStruct(tokens.shape, BF), in...  176 us
    unnamed x3, local copies, waits for them, and re-layouts  5 us

profile of v1, /device:TPU:0, one launch (start us, length us, event | category | flops | bytes accessed | tf_op | source)
XLA Modules:
  0.0 181.4 jit_solution(15233262006698795492)
XLA Ops:
  0.0 1.4 copy.8.refs_1_
  1.4 1.4 copy.9.refs_2_
  2.8 176.1 %shard_map.73 = bf16[2,64,3584]{2,1,0:T(8,128)(2,1)} custom-call(bf16[2,64,3584]{2,1,0:T(8,128)(2,1)} %refs_0_.1, s32[2,64,8]{2,1,0:T(8,128)} %copy.8.refs_1_, f32[2,64,8]{2,1,0:T(8,128)} %copy.9.refs_2_, s32[1,128]{1,0:T(1,128)} %bitcast.1, bf16[1,3584,1024]{2,1,0:T(8,128)(2,1)} %refs_4_.1, bf16[1,3584,1024]{2,1,0:T(8,128)(2,1)} %refs_5_.1, ...), custom_call_target="tpu_custom_call" | custom-call | flops 60000002048 | bytes 24000000 | tf_op jit(solution)/shard_map/pallas_call | solution.py:446
  178.9 2.2 %copy.11 = bf16[2,64,3584]{2,1,0:T(8,128)(2,1)} copy(bf16[2,64,3584]{2,1,0:T(8,128)(2,1)} %shard_map.73) | data formatting | bytes 1835008

commit v2 on v1

--- a/solution.py
+++ b/solution.py
@@ -44,8 +44,8 @@
     ex = lax.axis_index("expert")
     pos = (ex // 16, dp * 2 + (ex // 8) % 2, (ex // 2) % 4, ex % 2)
 
-    def cols(f):
-        return pl.ds(starts[f], widths[f])
+    def cols(m, f):
+        return pl.ds(starts[m][f], widths[m][f])
 
     def block(i, n):
         return pl.ds(pl.multiple_of(i * n, n), n)
@@ -61,12 +61,9 @@
     lane8 = lax.broadcasted_iota(I32, (8, 128), 1)
     twice = jnp.where(sub[:64] == lane[:64] % 64, 1.0, 0.0).astype(BF)
 
-    def turned(rows):
-        return lax.dot_general(rows.astype(BF), twice, (((0,), (0,)), ((), ())), preferred_element_type=F32)
-
     for m in range(batches):
-        names = turned(ids[m].astype(F32)).astype(I32)
-        gate_rows = turned(gates[m])
+        names = dot(ids[m].astype(F32).astype(BF), twice).astype(I32)
+        gate_rows = dot(gates[m].astype(BF), twice)
         same = [names[k : k + 1, :] == sub for k in range(8)]
         chosen = jnp.where(same[0], 1.0, 0.0)
         for k in range(1, 8):
@@ -113,8 +110,8 @@
     @once
     def phase1(m, f):
         b = AXES[f][0]
-        src = tokens.at[m, :, cols(f)]
-        dst = tok_all.at[m, pos[b], :, cols(f)]
+        src = tokens.at[m, :, cols(m, f)]
+        dst = tok_all.at[m, pos[b], :, cols(m, f)]
         far = [remote(src, dst, m, f, i, i, moved(pos, b, by)) for i, by in enumerate(RING)]
         return far, own(src, dst, m, f)
 
@@ -122,9 +119,9 @@
         a = AXES[f][1]
 
         def src(to):
-            return stage.at[m, block(to, 160), cols(f)]
-
-        dst = mid.at[m, block(pos[a], 160), cols(f)]
+            return stage.at[m, block(to, 160), cols(m, f)]
+
+        dst = mid.at[m, block(pos[a], 160), cols(m, f)]
         far = [
             remote(src((pos[a] + by) % 4), dst, m, f, i, base + i, moved(pos, a, by)) for i, by in enumerate(RING)
         ]
@@ -134,9 +131,9 @@
         a = AXES[f][2]
 
         def src(to, core):
-            return stage.at[m, block(core * 4 + to, 80), cols(f)]
-
-        dst = last.at[m, block(pos[3] * 4 + pos[a], 80), cols(f)]
+            return stage.at[m, block(core * 4 + to, 80), cols(m, f)]
+
+        dst = last.at[m, block(pos[3] * 4 + pos[a], 80), cols(m, f)]
         far = [
             remote(
                 src((pos[a] + by) % 4, 1 - pos[3] if dc else pos[3]), dst, m, f, i, base + i, moved(pos, a, by, dc)
@@ -166,7 +163,7 @@
         b = AXES[f][0]
         far = [
             remote(
-                tok_all.at[m, (pos[b] + by) % 4, :, cols(f)], fin.at[m, i, :, cols(f)], m, f, i, 23 + i,
+                tok_all.at[m, (pos[b] + by) % 4, :, cols(m, f)], fin.at[m, i, :, cols(m, f)], m, f, i, 23 + i,
                 moved(pos, b, by),
             )
             for i, by in enumerate(RING)
@@ -264,18 +261,18 @@
 
         lax.fori_loop(0, 2, one, 0)
 
-    def chunks(f):
+    def chunks(m, f):
         at = 0
-        while at < widths[f]:
-            size = min(512, widths[f] - at)
-            yield starts[f] + at, size
+        while at < widths[m][f]:
+            size = min(512, widths[m][f] - at)
+            yield starts[m][f] + at, size
             at += size
 
     def step1(m, f):
         build_pick(m, f)
         phase1(m, f)[1].wait()
         arrive((phase1(m, f)[0], None))
-        for at, size in chunks(f):
+        for at, size in chunks(m, f):
             rows = tok_all[m, :, :, at : at + size].reshape(4 * rows_tok, size)
             stage[m, :, at : at + size] = dot(pick[...], rows).astype(BF)
         sent(phase1(m, f))
@@ -286,7 +283,7 @@
         sent(phase2(m, f))
         @halves
         def _(c):
-            for at, size in chunks(f):
+            for at, size in chunks(m, f):
                 rows = jnp.concatenate(
                     [mid[m, block(i * 2 + c, 80), at : at + size] for i in range(4)], axis=0
                 )
@@ -308,7 +305,7 @@
         arrive(side(phase3(m, f), h))
         if h == 0:
             sent(phase3(m, f))
-        for at, size in chunks(f):
+        for at, size in chunks(m, f):
             rows = last[m, half(h), at : at + size]
             if f:
                 rows = dot((rot, rot_t)[f - 1][...], rows).astype(BF)
@@ -335,7 +332,7 @@
         rows = hidden[...]
         if f:
             rows = dot((rot_t, rot)[f - 1][...], rows).astype(BF)
-        for at, size in chunks(f):
+        for at, size in chunks(m, f):
             stage[m, half(h), at : at + size] = dot(rows, wd[:, at : at + size]).astype(BF)
         pl.semaphore_wait(free_last.at[m, f, h], 3 + h)
         start(side(back3(m, f), h))
@@ -345,7 +342,7 @@
         sent(back3(m, f))
         @halves
         def _(c):
-            for at, size in chunks(f):
+            for at, size in chunks(m, f):
                 rows = dot(swap[...], last[m, block(c, 320), at : at + size]).astype(BF)
                 for i in range(4):
                     stage[m, block(i * 2 + c, 80), at : at + size] = rows[i * 80 : i * 80 + 80, :]
@@ -356,21 +353,21 @@
     def step5(m, f):
         arrive(back2(m, f))
         sent(back2(m, f))
-        for at, size in chunks(f):
+        for at, size in chunks(m, f):
             rows = dot(comb[m, f], mid[m, :, at : at + size]).astype(BF)
             tok_all[m, :, :, at : at + size] = rows.reshape(4, rows_tok, size)
         start(back1(m, f))
 
     @once
     def leave(m, f):
-        return own(tok_all.at[m, pos[AXES[f][0]], :, cols(f)], out.at[m, :, cols(f)], m, f)
+        return own(tok_all.at[m, pos[AXES[f][0]], :, cols(m, f)], out.at[m, :, cols(m, f)], m, f)
 
     def step6(m, f):
         arrive(back1(m, f))
-        total = tok_all[m, pos[AXES[f][0]], :, cols(f)].astype(F32)
+        total = tok_all[m, pos[AXES[f][0]], :, cols(m, f)].astype(F32)
         for i in range(3):
-            total = total + fin[m, i, :, cols(f)].astype(F32)
-        tok_all[m, pos[AXES[f][0]], :, cols(f)] = total.astype(BF)
+            total = total + fin[m, i, :, cols(m, f)].astype(F32)
+        tok_all[m, pos[AXES[f][0]], :, cols(m, f)] = total.astype(BF)
         leave(m, f).start()
         sent(back1(m, f))
 
@@ -432,8 +429,9 @@
     ff = w_gate.shape[2]
     slots = 128 * CAP
     unit = width // 128
-    widths = (unit // 3 * 128, unit // 3 * 128, (unit - 2 * (unit // 3)) * 128)
-    starts = (0, widths[0], widths[0] + widths[1])
+    thin = unit // 3 * 128
+    widths = tuple((thin, width - 2 * thin, thin) if m % 2 else (thin, thin, width - 2 * thin) for m in range(batches))
+    starts = tuple((0, w[0], w[0] + w[1]) for w in widths)
     tile = 256
     tiles = ff // tile
 
@@ -475,7 +473,7 @@
         ],
         compiler_params=pltpu.CompilerParams(collective_id=0, has_side_effects=True, vmem_limit_bytes=62 << 20),
         cost_estimate=pl.CostEstimate(flops=60 * 10**9, bytes_accessed=24 * 10**6, transcendentals=10**6),
-    )(tokens, expert_ids, gate_weights, slot_expert.reshape(1, -1), w_gate, w_up, w_down)
+    )(tokens, jnp.swapaxes(expert_ids, 1, 2), jnp.swapaxes(gate_weights, 1, 2), slot_expert.reshape(1, -1), w_gate, w_up, w_down)
 
 
 def solution(mesh):

time: 184 us -> 179 us (0.973)
  local copies, waits for them, and re-layouts: 5 us -> 2.16 us
    unnamed x3 -> x1, local copies, waits for them, and re-layouts: 5 us -> 2.16 us
where the time goes in v2:
time: 179 us; the launch traced here: 177 us
  Pallas kernels  175 us (98%)
  local copies, waits for them, and re-layouts  2.16 us (1%)
    pallas_call x1, Pallas kernels, local(): pl.pallas_call(body, out_shape=jax.ShapeDtypeStruct(tokens.shape, BF), in...  175 us

profile of v2, /device:TPU:0, one launch (start us, length us, event | category | flops | bytes accessed | tf_op | source)
XLA Modules:
  0.0 176.9 jit_solution(7342371096757794617)
XLA Ops:
  0.0 174.6 %shard_map.73 = bf16[2,64,3584]{2,1,0:T(8,128)(2,1)} custom-call(bf16[2,64,3584]{2,1,0:T(8,128)(2,1)} %refs_0_.1, s32[2,8,64]{2,1,0:T(8,128)} %bitcast.3, f32[2,8,64]{2,1,0:T(8,128)} %bitcast.4, s32[1,128]{1,0:T(1,128)} %bitcast.5, bf16[1,3584,1024]{2,1,0:T(8,128)(2,1)} %refs_4_.1, bf16[1,3584,1024]{2,1,0:T(8,128)(2,1)} %refs_5_.1, ...), custom_call_target="tpu_custom_call" | custom-call | flops 60000002048 | bytes 24000000 | tf_op jit(solution)/shard_map/pallas_call | solution.py:444
  174.6 2.2 %copy.9 = bf16[2,64,3584]{2,1,0:T(8,128)(2,1)} copy(bf16[2,64,3584]{2,1,0:T(8,128)(2,1)} %shard_map.73) | data formatting | bytes 1835008

commit v3 on v2

--- a/solution.py
+++ b/solution.py
@@ -112,7 +112,7 @@
         b = AXES[f][0]
         src = tokens.at[m, :, cols(m, f)]
         dst = tok_all.at[m, pos[b], :, cols(m, f)]
-        far = [remote(src, dst, m, f, i, i, moved(pos, b, by)) for i, by in enumerate(RING)]
+        far = [remote(src, dst, m, f, 3 + i, i, moved(pos, b, by)) for i, by in enumerate(RING)]
         return far, own(src, dst, m, f)
 
     def along_mid(m, f, base):
@@ -163,7 +163,7 @@
         b = AXES[f][0]
         far = [
             remote(
-                tok_all.at[m, (pos[b] + by) % 4, :, cols(m, f)], fin.at[m, i, :, cols(m, f)], m, f, i, 23 + i,
+                tok_all.at[m, (pos[b] + by) % 4, :, cols(m, f)], fin.at[m, i, :, cols(m, f)], m, f, 3 + i, 23 + i,
                 moved(pos, b, by),
             )
             for i, by in enumerate(RING)
@@ -275,11 +275,11 @@
         for at, size in chunks(m, f):
             rows = tok_all[m, :, :, at : at + size].reshape(4 * rows_tok, size)
             stage[m, :, at : at + size] = dot(pick[...], rows).astype(BF)
-        sent(phase1(m, f))
         start(phase2(m, f))
 
     def step2(m, f):
         arrive(phase2(m, f))
+        sent(phase1(m, f))
         sent(phase2(m, f))
         @halves
         def _(c):
@@ -352,7 +352,6 @@
 
     def step5(m, f):
         arrive(back2(m, f))
-        sent(back2(m, f))
         for at, size in chunks(m, f):
             rows = dot(comb[m, f], mid[m, :, at : at + size]).astype(BF)
             tok_all[m, :, :, at : at + size] = rows.reshape(4, rows_tok, size)
@@ -369,6 +368,7 @@
             total = total + fin[m, i, :, cols(m, f)].astype(F32)
         tok_all[m, pos[AXES[f][0]], :, cols(m, f)] = total.astype(BF)
         leave(m, f).start()
+        sent(back2(m, f))
         sent(back1(m, f))
 
     parts = range(3)
@@ -379,11 +379,11 @@
     for f in parts:
         build_comb(0, f)
     for f in parts:
+        step2(0, f)
+    for f in parts:
+        step2(1, f)
+    for f in parts:
         build_comb(1, f)
-    for f in parts:
-        step2(0, f)
-    for f in parts:
-        step2(1, f)
     for copy in loads:
         copy.wait()
     for f in parts:

time: 179 us -> 180 us (level)
  no operation moved by 1% of the time
where the time goes in v3:
time: 180 us; the launch traced here: 177 us
  Pallas kernels  175 us (97%)
  local copies, waits for them, and re-layouts  2.16 us (1%)
    pallas_call x1, Pallas kernels, local(): pl.pallas_call(body, out_shape=jax.ShapeDtypeStruct(tokens.shape, BF), in...  175 us

profile of v3, /device:TPU:0, one launch (start us, length us, event | category | flops | bytes accessed | tf_op | source)
XLA Modules:
  0.0 177.1 jit_solution(14936746350260125707)
XLA Ops:
  0.0 174.6 %shard_map.73 = bf16[2,64,3584]{2,1,0:T(8,128)(2,1)} custom-call(bf16[2,64,3584]{2,1,0:T(8,128)(2,1)} %refs_0_.1, s32[2,8,64]{2,1,0:T(8,128)} %bitcast.3, f32[2,8,64]{2,1,0:T(8,128)} %bitcast.4, s32[1,128]{1,0:T(1,128)} %bitcast.5, bf16[1,3584,1024]{2,1,0:T(8,128)(2,1)} %refs_4_.1, bf16[1,3584,1024]{2,1,0:T(8,128)(2,1)} %refs_5_.1, ...), custom_call_target="tpu_custom_call" | custom-call | flops 60000002048 | bytes 24000000 | tf_op jit(solution)/shard_map/pallas_call | solution.py:444
  174.6 2.2 %copy.9 = bf16[2,64,3584]{2,1,0:T(8,128)(2,1)} copy(bf16[2,64,3584]{2,1,0:T(8,128)(2,1)} %shard_map.73) | data formatting | bytes 1835008
